TPU v7x, 32 devices: a whole 2x2x4 slice. The times are simulated.
32 devices in a mesh: gx: 8 (over z, core), gy: 4 (over y, x).
Axes of the slice: x: 2, y: 2, z: 4, core: 2. Of those that a mesh axis runs over, the one named last changes fastest.
Arguments:
- masses: bfloat16 [256, 32, 32, 128], P(None, 'gx', 'gy'), may hold values from 0 to 1
- table: bfloat16 [256, 17], replicated, may hold values from 0.0009994507 to 0.019897461
- star_mask: int32 [32, 32, 128], P('gx', 'gy'), may hold values 0 or 1
- density: float32 [32, 32, 128], P('gx', 'gy'), may hold values from 0.1 to 10
- metals: float32 [16, 32, 32, 128], P(None, 'gx', 'gy'), may hold values from 0.1 to 1
- energy: float32 [32, 32, 128], P('gx', 'gy'), may hold values from 0.5 to 2
- courant_x: float32 [32, 32, 128], P('gx', 'gy'), may hold values from -0.3 to 0.3
- courant_y: float32 [32, 32, 128], P('gx', 'gy'), may hold values from -0.3 to 0.3
- courant_z: float32 [32, 32, 128], P('gx', 'gy'), may hold values from -0.3 to 0.3
Outputs:
- advected: float32 [16, 32, 32, 128], P(None, 'gx', 'gy')
- energy_out: float32 [32, 32, 128], P('gx', 'gy')
Inputs may be any that keep to these rules, and one draw needn't show every extreme that they name: `star_mask`: 1 marks a star-forming cell, 0 any other.
All inputs are finite; a program needn't handle non-finite values. No bound on the sum of `star_mask` on one device may be relied on, other than what follows from the above.
Results may differ from a plain program's by a relative error of at most 0.0003.
Values sent between devices are 32-bit elements; how exact they have to be, the bound alone decides.
No kernel may reach another device: no remote copies, remote signals or barrier semaphores. Data moves between devices by JAX's collectives and lax.ppermute only.
A program may use at most 64 MiB of HBM per device.

v0:
```python
import jax
import jax.numpy as jnp
from jax import lax
from jax.experimental import pallas as pl
from jax.experimental.pallas import tpu as pltpu
from jax.sharding import PartitionSpec as P

F32 = jnp.float32
BF16 = jnp.bfloat16
BINS = 256
COMP = 17
NMET = 16
BX = 4
BY = 8
NZ = 128
CHUNKS = 4
GROUP = 4
YROWS = 112
ZROWS = 114
XROWS = 424
CROWS = 114
PITCH = 24
DENSITIES = [(w, q) for w in range(3) for q in range(3) if w + q < 4]
DPITCH = 40


def rows(start, count, stride=1):
    return pl.ds(start, count) if stride == 1 else pl.ds(start, count, stride)


def place(axis):
    index = lax.axis_index(axis)
    last = index == lax.axis_size(axis) - 1
    odd = index % 2
    alone_a = jnp.logical_and(odd == 0, last)
    alone_b = jnp.logical_or(index == 0, jnp.logical_and(odd == 1, last))
    return 1 - odd, alone_a, alone_b


def sources_kernel(
    masses_hbm, table_hbm, star_hbm, dens_hbm, metals_hbm, energy_hbm, cx_hbm, cy_hbm, cz_hbm,
    src_ref, ya_ref, yb_ref, xa_ref, xb_ref, za_ref, zb_ref,
    dens_ref, metals_ref, energy_ref, cx_ref, cy_ref, cz_ref,
    mass_buf, table_ref, star_ref, expand_ref, wide_ref, mass_sems, sems,
):
    small = [
        (table_hbm, table_ref), (star_hbm, star_ref), (dens_hbm, dens_ref), (metals_hbm, metals_ref),
        (cx_hbm, cx_ref), (cy_hbm, cy_ref), (cz_hbm, cz_ref), (energy_hbm, energy_ref),
    ]
    small_copies = [
        pltpu.make_async_copy(hbm, ref, sems.at[i]) for i, (hbm, ref) in enumerate(small)
    ]
    per = BINS // CHUNKS
    copies = [
        pltpu.make_async_copy(
            masses_hbm.at[pl.ds(c * per, per)], mass_buf.at[pl.ds(c * per, per)], mass_sems.at[c]
        )
        for c in range(CHUNKS)
    ]
    small_copies[0].start()
    for copy in copies:
        copy.start()
    for copy in small_copies[1:]:
        copy.start()

    width = BINS * BY
    group = lax.broadcasted_iota(jnp.int32, (8, NZ), 1) // BY
    same = (
        lax.broadcasted_iota(jnp.int32, (BY, NZ), 1) % BY
        == lax.broadcasted_iota(jnp.int32, (BY, NZ), 0)
    )
    upper = lax.broadcasted_iota(jnp.int32, (1, 16, NZ), 1) < BY
    small_copies[0].wait()
    turned = table_ref[...].astype(F32)
    turned = jnp.concatenate([turned, jnp.zeros((24 - COMP, BINS), F32)], axis=0)

    def expand(c):
        tiles = width // NZ // CHUNKS
        for t in range(c * tiles, (c + 1) * tiles):
            first = 16 * t
            half = first // NZ
            columns = slice(t * NZ, (t + 1) * NZ)
            for r in range(3):
                tile = turned[8 * r : 8 * r + 8, half * NZ : (half + 1) * NZ]
                wide_ref[8 * r : 8 * r + 8, columns] = jnp.take_along_axis(
                    tile, group + first % NZ, axis=1
                )
            for k in range(0, COMP + 1, 2):
                lines = [
                    jnp.where(same, jnp.broadcast_to(wide_ref[i : i + 1, columns], (BY, NZ)), 0.0)
                    for i in (k, k + 1)
                ]
                expand_ref[k * BY : k * BY + 16, columns] = jnp.concatenate(lines, axis=0).astype(BF16)

    expand(0)
    total = None
    for c in range(CHUNKS):
        copies[c].wait()
        part = mass_buf[c * per : (c + 1) * per]
        blocks = []
        for j in range(2):
            both = part[:, 16 * j : 16 * j + 16].reshape(per // 2, 2, 16, NZ)
            even, odd = both[:, 0], both[:, 1]
            blocks.append(jnp.where(upper, even, pltpu.roll(odd, 8, 1)).reshape(per * BY, NZ))
            blocks.append(jnp.where(upper, pltpu.roll(even, 8, 1), odd).reshape(per * BY, NZ))
        right = jnp.concatenate(blocks, axis=1)
        left = expand_ref[:, c * per * BY : (c + 1) * per * BY]
        prod = jnp.dot(left, right, preferred_element_type=F32)
        total = prod if total is None else total + prod
        if c + 1 < CHUNKS:
            expand(c + 1)
    for copy in small_copies[1:]:
        copy.wait()
    for x in range(BX):
        mask = star_ref[x * BY : x * BY + BY, :].astype(F32)
        for k in range(COMP):
            at = (k * BX + x) * BY
            piece = total[k * BY : k * BY + BY, x * NZ : (x + 1) * NZ]
            src_ref[at : at + BY, :] = piece * mask

    even_x, alone_xa, alone_xb = place("gx")
    even_y, alone_ya, alone_yb = place("gy")
    plane = BX * BY
    for out, rest, high in ((ya_ref, za_ref, even_y), (yb_ref, zb_ref, 1 - even_y)):
        near = jnp.where(high == 1, BY - 1, 0)
        step = jnp.where(high == 1, -1, 1)
        out[0:64, :] = src_ref[rows(near, 64, BY), :]
        for i, x in enumerate((0, BX - 1)):
            out[64 + 16 * i : 80 + 16 * i, :] = src_ref[rows(x * BY + near + step, 16, plane), :]
        out[96:100, :] = src_ref[rows(NMET * plane + near, 4, BY), :]
        out[100:104, :] = dens_ref[rows(near, 4, BY), :]
        out[104:108, :] = dens_ref[rows(near + step, 4, BY), :]
        out[108:112, :] = dens_ref[rows(near + 2 * step, 4, BY), :]
        rest[0:64, :] = metals_ref[rows(near, 64, BY), :]
        for x in range(1, BX - 1):
            at = 64 + 16 * (x - 1)
            rest[at : at + 16, :] = src_ref[rows(x * BY + near + step, 16, plane), :]
        rest[96:100, :] = cy_ref[rows(near, 4, BY), :]
        rest[100:ZROWS, :] = jnp.zeros((ZROWS - 100, NZ), F32)
    for out, high in ((xa_ref, even_x), (xb_ref, 1 - even_x)):
        near = jnp.where(high == 1, BX - 1, 0) * BY
        step = jnp.where(high == 1, -1, 1) * BY
        tile = 0
        pieces = [(src_ref, k * BX * BY + near) for k in range(COMP)]
        pieces += [(src_ref, k * BX * BY + near + step) for k in range(NMET)]
        pieces += [(metals_ref, k * BX * BY + near) for k in range(NMET)]
        pieces += [(dens_ref, near), (dens_ref, near + step), (dens_ref, near + 2 * step)]
        pieces += [(cx_ref, near)]
        for ref, at in pieces:
            out[tile * BY : tile * BY + BY, :] = ref[pl.ds(pl.multiple_of(at, BY), BY), :]
            tile += 1
    for out, alone in (
        (ya_ref, alone_ya), (yb_ref, alone_yb), (za_ref, alone_ya), (zb_ref, alone_yb),
        (xa_ref, alone_xa), (xb_ref, alone_xb),
    ):
        clear(out, alone)


def clear(ref, alone):
    @pl.when(alone)
    def _():
        ref[...] = jnp.zeros(ref.shape, F32)


def corner_kernel(ya_ref, yb_ref, xa_ref, xb_ref, ca_ref, cb_ref):
    del xa_ref, xb_ref
    even_x, alone_a, alone_b = place("gx")
    for out, high in ((ca_ref, even_x), (cb_ref, 1 - even_x)):
        near = jnp.where(high == 1, BX - 1, 0)
        step = jnp.where(high == 1, -1, 1)
        at = pl.multiple_of(jnp.where(high == 1, 80, 64), 16)
        for side, y_ref in enumerate((ya_ref, yb_ref)):
            base = side * 48
            out[base : base + 16, :] = y_ref[rows(near, 16, BX), :]
            out[base + 16 : base + 32, :] = y_ref[rows(near + step, 16, BX), :]
            out[base + 32 : base + 48, :] = y_ref[pl.ds(at, 16), :]
            base = 96 + side * 9
            out[base : base + 1, :] = y_ref[pl.ds(96 + near, 1), :]
            for i, (w, q) in enumerate(DENSITIES):
                out[base + 1 + i : base + 2 + i, :] = y_ref[pl.ds(100 + 4 * w + near + q * step, 1), :]
    clear(ca_ref, alone_a)
    clear(cb_ref, alone_b)


def sort_kernel(za_ref, zb_ref, zlow_ref, zhigh_ref):
    a_is_high = place("gy")[0] == 1
    a = za_ref[...]
    b = zb_ref[...]
    zlow_ref[...] = jnp.where(a_is_high, b, a)
    zhigh_ref[...] = jnp.where(a_is_high, a, b)


def finish_kernel(
    src_ref, ya_ref, yb_ref, xa_ref, xb_ref, zlow_ref, zhigh_ref, ca_ref, cb_ref,
    dens_ref, metals_ref, energy_ref, cx_ref, cy_ref, cz_ref,
    out_hbm, energy_out_hbm,
    out_ref, energy_out_ref, sems,
    se_ref, de_ref, rw_ref, ys_ref, ee_ref, mx_ref, my_ref, cxl_ref, cye_ref,
):
    even_x = place("gx")[0]
    even_y = place("gy")[0]
    lane = lax.broadcasted_iota(jnp.int32, (1, NZ), 1)
    not_first = lane > 0
    not_last = lane < NZ - 1

    def prev_z(v):
        return pltpu.roll(v, 1, 1)

    def next_z(v):
        return pltpu.roll(v, NZ - 1, 1)

    def masked_prev(v):
        return jnp.where(not_first, prev_z(v), 0.0)

    def masked_next(v):
        return jnp.where(not_last, next_z(v), 0.0)

    de_ref[...] = jnp.zeros(de_ref.shape, F32)

    for x in range(BX):
        at = x * BY
        d_at = (x + 3) * DPITCH + 16
        de_ref[d_at : d_at + BY, :] = dens_ref[at : at + BY, :]
        cye_ref[x * PITCH + 8 : x * PITCH + 16, :] = cy_ref[at : at + BY, :]
        for k in range(COMP):
            s_at = (k * 8 + x + 2) * PITCH + 8
            se_ref[s_at : s_at + BY, :] = src_ref[(k * BX + x) * BY : (k * BX + x + 1) * BY, :]

    for y_ref, high in ((ya_ref, even_y), (yb_ref, 1 - even_y)):
        is_high = high == 1
        r1 = jnp.where(is_high, 16, 7)
        r2 = jnp.where(is_high, 17, 6)
        for k in range(NMET):
            at = k * BX
            base = (k * 8 + 2) * PITCH
            se_ref[rows(base + r1, BX, PITCH), :] = y_ref[at : at + BX, :]
        for i, x in enumerate((0, BX - 1)):
            se_ref[rows((x + 2) * PITCH + r2, NMET, 8 * PITCH), :] = y_ref[64 + 16 * i : 80 + 16 * i, :]
        base = (NMET * 8 + 2) * PITCH
        se_ref[rows(base + r1, BX, PITCH), :] = y_ref[96:100, :]
        for w in range(3):
            d_row = jnp.where(is_high, 24 + w, 15 - w)
            de_ref[rows(3 * DPITCH + d_row, BX, DPITCH), :] = y_ref[100 + 4 * w : 104 + 4 * w, :]
    for side, z_ref in enumerate((zlow_ref, zhigh_ref)):
        for k in range(NMET):
            my_ref[side, k * 8 + 2 : k * 8 + 2 + BX, :] = z_ref[k * BX : k * BX + BX, :]
        for x in range(1, BX - 1):
            r2 = (6, 17)[side]
            se_ref[rows((x + 2) * PITCH + r2, NMET, 8 * PITCH), :] = z_ref[48 + 16 * x : 64 + 16 * x, :]
    cye_ref[rows(7, BX, PITCH), :] = zlow_ref[96:100, :]

    for x_ref, c_ref, high in ((xa_ref, ca_ref, even_x), (xb_ref, cb_ref, 1 - even_x)):
        is_high = high == 1
        p1 = jnp.where(is_high, 6, 1)
        p2 = jnp.where(is_high, 7, 0)
        for k in range(COMP):
            at = pl.multiple_of((k * 8 + p1) * PITCH + 8, 8)
            se_ref[pl.ds(at, BY), :] = x_ref[k * BY : k * BY + BY, :]
        for k in range(NMET):
            at = pl.multiple_of((k * 8 + p2) * PITCH + 8, 8)
            tile = COMP + k
            se_ref[pl.ds(at, BY), :] = x_ref[tile * BY : tile * BY + BY, :]
            tile = COMP + NMET + k
            mx_ref[high, k * BY : k * BY + BY, :] = x_ref[tile * BY : tile * BY + BY, :]
        for w in range(3):
            tile = COMP + 2 * NMET + w
            plane = jnp.where(is_high, 7 + w, 2 - w)
            at = pl.multiple_of(plane * DPITCH + 16, 8)
            de_ref[pl.ds(at, BY), :] = x_ref[tile * BY : tile * BY + BY, :]
        tile = COMP + 2 * NMET + 3
        cxl_ref[high] = x_ref[tile * BY : tile * BY + BY, :]
        for side, y_high in enumerate((even_y, 1 - even_y)):
            base = 48 * side
            y_is_high = y_high == 1
            r1 = jnp.where(y_is_high, 16, 7)
            r2 = jnp.where(y_is_high, 17, 6)
            se_ref[rows(p1 * PITCH + r1, NMET, 8 * PITCH), :] = c_ref[base : base + 16, :]
            se_ref[rows(p2 * PITCH + r1, NMET, 8 * PITCH), :] = c_ref[base + 16 : base + 32, :]
            se_ref[rows(p1 * PITCH + r2, NMET, 8 * PITCH), :] = c_ref[base + 32 : base + 48, :]
            base = 96 + 9 * side
            se_ref[pl.ds((NMET * 8 + p1) * PITCH + r1, 1), :] = c_ref[base : base + 1, :]
            for i, (w, q) in enumerate(DENSITIES):
                d_row = jnp.where(y_is_high, 24 + w, 15 - w)
                plane = jnp.where(is_high, 7 + q, 2 - q)
                de_ref[pl.ds(plane * DPITCH + d_row, 1), :] = c_ref[base + 1 + i : base + 2 + i, :]

    columns = []
    for p in range(10):
        at = p * DPITCH + 8
        columns.append(
            de_ref[at - 1 : at + 23, :] + de_ref[at : at + 24, :] + de_ref[at + 1 : at + 25, :]
        )
    for p in range(8):
        flat = columns[p] + columns[p + 1] + columns[p + 2]
        weight = flat + masked_prev(flat) + masked_next(flat)
        inside = weight > 0.0
        rw_ref[p * PITCH : (p + 1) * PITCH, :] = jnp.where(
            inside, 1.0 / jnp.where(inside, weight, 1.0), 0.0
        )

    copies = []
    for first in range(NMET, -1, -GROUP):
        group = [first] if first == NMET else range(first, first + GROUP)
        share_sums(group, se_ref, rw_ref, ys_ref)
        for k in group:
            for p in range(2, 6) if k == NMET else range(1, 7):
                dens = de_ref[(p + 1) * DPITCH + 16 : (p + 1) * DPITCH + 24, :]
                at = (k * 8 + p) * BY
                flat = (
                    ys_ref[at - BY : at, :] + ys_ref[at : at + BY, :] + ys_ref[at + BY : at + 2 * BY, :]
                )
                collected = flat + masked_prev(flat) + masked_next(flat)
                deposit = dens * collected
                if k == NMET:
                    cell = (p - 2) * BY
                    energy_out_ref[cell : cell + BY, :] = energy_ref[cell : cell + BY, :] + deposit
                    continue
                if p == 1:
                    metal = mx_ref[0, k * BY : k * BY + BY, :]
                elif p == 6:
                    metal = mx_ref[1, k * BY : k * BY + BY, :]
                else:
                    cell = (k * BX + p - 2) * BY
                    metal = metals_ref[cell : cell + BY, :]
                e_at = (k * 8 + p) * PITCH + 8
                ee_ref[e_at : e_at + BY, :] = metal + deposit
        if first == NMET:
            copies.append(pltpu.make_async_copy(energy_out_ref, energy_out_hbm, sems.at[0]))
            copies[-1].start()
            continue

        for side in range(2):
            row = (7, 16)[side]
            dens = de_ref[rows(DPITCH + row + 8, 8, DPITCH), :]
            inv = [rw_ref[rows(row - 1 + d, 8, PITCH), :] for d in range(3)]
            for k in group:
                value = None
                for d in range(3):
                    term = se_ref[rows(k * 8 * PITCH + row - 1 + d, 8, PITCH), :] * inv[d]
                    value = term if value is None else value + term
                flat = value + pltpu.roll(value, 1, 0) + pltpu.roll(value, 7, 0)
                deposit = dens * (flat + masked_prev(flat) + masked_next(flat))
                ee_ref[rows(k * 8 * PITCH + row, 8, PITCH), :] = (
                    my_ref[side, k * 8 : k * 8 + 8, :] + deposit
                )

        for x in range(BX):
            at = x * BY
            cx_up = cx_ref[at : at + BY, :]
            cx_low = cxl_ref[0] if x == 0 else cx_ref[at - BY : at, :]
            cy_up = cy_ref[at : at + BY, :]
            cy_low = cye_ref[x * PITCH + 7 : x * PITCH + 15, :]
            cz_up = cz_ref[at : at + BY, :]
            cz_low = masked_prev(cz_up)
            to_next = [-jnp.minimum(c, 0.0) for c in (cx_up, cy_up, cz_up)]
            from_prev = [jnp.maximum(c, 0.0) for c in (cx_low, cy_low, cz_low)]
            middle = 1.0
            for up, low in ((cx_up, cx_low), (cy_up, cy_low), (cz_up, cz_low)):
                middle = middle - jnp.maximum(up, 0.0) + jnp.minimum(low, 0.0)
            to_next[2] = jnp.where(not_last, to_next[2], 0.0)
            for k in group:
                e_at = (k * 8 + x + 2) * PITCH + 8
                own = ee_ref[e_at : e_at + BY, :]
                result = middle * own
                result = result + to_next[0] * ee_ref[e_at + PITCH : e_at + PITCH + BY, :]
                result = result + from_prev[0] * ee_ref[e_at - PITCH : e_at - PITCH + BY, :]
                result = result + to_next[1] * ee_ref[e_at + 1 : e_at + 1 + BY, :]
                result = result + from_prev[1] * ee_ref[e_at - 1 : e_at - 1 + BY, :]
                result = result + to_next[2] * next_z(own)
                result = result + from_prev[2] * prev_z(own)
                cell = (k * BX + x) * BY
                out_ref[cell : cell + BY, :] = result
        piece = pl.ds(first * BX * BY, GROUP * BX * BY)
        copies.append(
            pltpu.make_async_copy(out_ref.at[piece], out_hbm.at[piece], sems.at[len(copies)])
        )
        copies[-1].start()
    for copy in copies:
        copy.wait()


def share_sums(group, se_ref, rw_ref, ys_ref):
    for p in range(8):
        inv = [rw_ref[p * PITCH + 7 + d : p * PITCH + 15 + d, :] for d in range(3)]
        for k in group:
            if k == NMET and p in (0, 7):
                continue
            at = (k * 8 + p) * PITCH + 7
            value = None
            for d in range(3):
                term = se_ref[at + d : at + d + BY, :] * inv[d]
                value = term if value is None else value + term
            ys_ref[(k * 8 + p) * BY : (k * 8 + p) * BY + BY, :] = value


def swaps():
    nx = lax.axis_size("gx")
    ny = lax.axis_size("gy")
    rounds = []
    for along_x in (True, False):
        for first in (0, 1):
            pairs = []
            for x in range(nx):
                for y in range(ny):
                    place_, count = (x, nx) if along_x else (y, ny)
                    mate = place_ + 1 if place_ % 2 == first else place_ - 1
                    if 0 <= mate < count:
                        to = (mate, y) if along_x else (x, mate)
                    elif along_x and ny % 2 == 0:
                        to = (x, (y + ny // 2) % ny)
                    elif not along_x and nx % 2 == 0:
                        to = (x + 1 - 2 * (x % 2), y)
                    else:
                        to = (x, y)
                    pairs.append((x * ny + y, to[0] * ny + to[1]))
            rounds.append(pairs)
    return rounds


def swap(value, pairs):
    return lax.ppermute(value, ("gx", "gy"), pairs)


VM = pl.BlockSpec(memory_space=pltpu.VMEM)
HB = pl.BlockSpec(memory_space=pltpu.HBM)


def buffer(count):
    return pltpu.VMEM((count, NZ), F32)


def body(masses, table, star_mask, density, metals, energy, courant_x, courant_y, courant_z):
    cells = BX * BY
    masses = masses.reshape(BINS, cells, NZ)
    star_mask, density, energy, courant_x, courant_y, courant_z = (
        a.reshape(cells, NZ) for a in (star_mask, density, energy, courant_x, courant_y, courant_z)
    )
    metals = metals.reshape(NMET * cells, NZ)
    src, ya, yb, xa, xb, za, zb, *local = pl.pallas_call(
        sources_kernel,
        name="sources",
        out_shape=[buffer(COMP * cells)]
        + [buffer(count) for count in (YROWS, YROWS, XROWS, XROWS, ZROWS, ZROWS)]
        + [buffer(cells), buffer(NMET * cells)] + [buffer(cells)] * 4,
        in_specs=[HB] * 9,
        out_specs=[VM] * 13,
        scratch_shapes=[
            pltpu.VMEM((BINS, cells, NZ), BF16),
            pltpu.VMEM((COMP, BINS), BF16),
            pltpu.VMEM((cells, NZ), jnp.int32),
            pltpu.VMEM(((COMP + 1) * BY, BINS * BY), BF16),
            pltpu.VMEM((24, BINS * BY), F32),
            pltpu.SemaphoreType.DMA((CHUNKS,)),
            pltpu.SemaphoreType.DMA((8,)),
        ],
        compiler_params=pltpu.CompilerParams(vmem_limit_bytes=32 * 1024 * 1024),
    )(
        *(
            pltpu.with_memory_space_constraint(a, pltpu.HBM)
            for a in (
                masses, table.T, star_mask, density, metals, energy, courant_x, courant_y, courant_z
            )
        )
    )
    pairs_xa, pairs_xb, pairs_ya, pairs_yb = swaps()
    ya = swap(ya, pairs_ya)
    yb = swap(yb, pairs_yb)
    xa = swap(xa, pairs_xa)
    xb = swap(xb, pairs_xb)
    za = swap(za, pairs_ya)
    zb = swap(zb, pairs_yb)
    ca, cb = pl.pallas_call(
        corner_kernel,
        name="corners",
        out_shape=[buffer(CROWS), buffer(CROWS)],
        in_specs=[VM] * 4,
        out_specs=[VM, VM],
        compiler_params=pltpu.CompilerParams(vmem_limit_bytes=4 * 1024 * 1024),
    )(*(pltpu.with_memory_space_constraint(a, pltpu.VMEM) for a in (ya, yb, xa, xb)))
    ca = swap(ca, pairs_xa)
    cb = swap(cb, pairs_xb)
    z = pl.pallas_call(
        sort_kernel,
        name="sort",
        out_shape=[buffer(ZROWS), buffer(ZROWS)],
        in_specs=[VM] * 2,
        out_specs=[VM] * 2,
        compiler_params=pltpu.CompilerParams(vmem_limit_bytes=4 * 1024 * 1024),
    )(*(pltpu.with_memory_space_constraint(a, pltpu.VMEM) for a in (za, zb)))
    advected, energy_out = pl.pallas_call(
        finish_kernel,
        name="finish",
        out_shape=[
            jax.ShapeDtypeStruct((NMET * cells, NZ), F32),
            jax.ShapeDtypeStruct((cells, NZ), F32),
        ],
        in_specs=[VM] * 15,
        out_specs=[HB, HB],
        scratch_shapes=[
            pltpu.VMEM((NMET * cells, NZ), F32),
            pltpu.VMEM((cells, NZ), F32),
            pltpu.SemaphoreType.DMA((1 + NMET // GROUP,)),
            pltpu.VMEM((COMP * 8 * PITCH, NZ), F32),
            pltpu.VMEM((10 * DPITCH, NZ), F32),
            pltpu.VMEM((8 * PITCH, NZ), F32),
            pltpu.VMEM((COMP * 8 * BY, NZ), F32),
            pltpu.VMEM((NMET * 8 * PITCH, NZ), F32),
            pltpu.VMEM((2, NMET * BY, NZ), F32),
            pltpu.VMEM((2, NMET * 8, NZ), F32),
            pltpu.VMEM((2, BY, NZ), F32),
            pltpu.VMEM((BX * PITCH, NZ), F32),
        ],
        compiler_params=pltpu.CompilerParams(vmem_limit_bytes=32 * 1024 * 1024),
    )(
        *(
            pltpu.with_memory_space_constraint(a, pltpu.VMEM)
            for a in (src, ya, yb, xa, xb, *z, ca, cb, *local)
        )
    )
    return advected.reshape(NMET, BX, BY, NZ), energy_out.reshape(BX, BY, NZ)


def solution(mesh):
    field = P("gx", "gy", None)
    stack = P(None, "gx", "gy", None)
    in_specs = (stack, P(), field, field, stack, field, field, field, field)
    out_specs = (stack, field)
    return jax.shard_map(body, mesh=mesh, in_specs=in_specs, out_specs=out_specs, check_vma=False)
```

profile of v0, /device:TPU:0, one launch (start us, length us, event | category | flops | bytes accessed | tf_op | source)
XLA Modules:
  0.0 17.8 jit_solution(9858945921623805686)
XLA Ops:
  0.6 2.3 %sources.1 = (f32[544,128]{1,0:T(8,128)S(1)}, f32[112,128]{1,0:T(8,128)S(1)}, f32[112,128]{1,0:T(8,128)S(1)}, f32[424,128]{1,0:T(8,128)S(1)}, f32[424,128]{1,0:T...) custom-call(bf16[256,32,128]{2,1,0:T(8,128)(2,1)} %bitcast.11, ...), custom_call_target="tpu_custom_call" | custom-call | tf_op jit(solution)/shard_map/sources/pallas_call | solution.py:439
  3.0 0.5 %collective-permute-start.2 = (f32[424,128]{1,0:T(8,128)S(1)}, f32[424,128]{1,0:T(8,128)S(1)}, u32[]{:S(2)}, u32[]{:S(2)}) collective-permute-start(f32[424,128]{1,0:T(8,128)S(1)} %get-tuple-element.24), channel_id=1, source_target_pairs={{0,4},{1,5},{2,6},{3,7},{4,0},{5,1},{6,2},{7,3},{8,12},{9,13},{10,... | collective-permute-start | bytes 651272 | tf_op jit(solution)/shard_map/ppermute | solution.py:421
  3.5 2.6 %collective-permute-start.3 = (f32[424,128]{1,0:T(8,128)S(1)}, f32[424,128]{1,0:T(8,128)S(1)}, u32[]{:S(2)}, u32[]{:S(2)}) collective-permute-start(f32[424,128]{1,0:T(8,128)S(1)} %get-tuple-element.25), channel_id=1, source_target_pairs={{0,2},{1,3},{2,0},{3,1},{4,8},{5,9},{6,10},{7,11},{8,4},{9,5},{10,... | collective-permute-start | bytes 651272 | tf_op jit(solution)/shard_map/ppermute | solution.py:421
  6.1 1.5 %collective-permute-start = (f32[112,128]{1,0:T(8,128)S(1)}, f32[112,128]{1,0:T(8,128)S(1)}, u32[]{:S(2)}, u32[]{:S(2)}) collective-permute-start(f32[112,128]{1,0:T(8,128)S(1)} %get-tuple-element.22), channel_id=1, source_target_pairs={{0,1},{1,0},{2,3},{3,2},{4,5},{5,4},{6,7},{7,6},{8,9},{9,8},{10,11... | collective-permute-start | bytes 172040 | tf_op jit(solution)/shard_map/ppermute | solution.py:421
  7.6 0.0 collective-permute-start.1
  7.6 2.0 %collective-permute-start.4 = (f32[114,128]{1,0:T(8,128)S(1)}, f32[114,128]{1,0:T(8,128)S(1)}, u32[]{:S(2)}, u32[]{:S(2)}) collective-permute-start(f32[114,128]{1,0:T(8,128)S(1)} %get-tuple-element.26), channel_id=1, source_target_pairs={{0,1},{1,0},{2,3},{3,2},{4,5},{5,4},{6,7},{7,6},{8,9},{9,8},{10,11... | collective-permute-start | bytes 175112 | tf_op jit(solution)/shard_map/ppermute | solution.py:421
  9.5 0.7 %collective-permute-done.ya_ref = f32[112,128]{1,0:T(8,128)S(1)} collective-permute-done((f32[112,128]{1,0:T(8,128)S(1)}, f32[112,128]{1,0:T(8,128)S(1)}, u32[]{:S(2)}, u32[]{:S(2)}) %collective-permute-start) | collective-permute-done | bytes 57376 | tf_op jit(solution)/shard_map/ppermute | solution.py:421
  10.3 0.0 collective-permute-start.5
  10.3 0.0 collective-permute-done.1.yb_ref
  10.3 0.0 collective-permute-done.2.xa_ref
  10.3 0.0 collective-permute-done.3.xb_ref
  10.3 0.6 %collective-permute-start.6 = (f32[114,128]{1,0:T(8,128)S(1)}, f32[114,128]{1,0:T(8,128)S(1)}, u32[]{:S(2)}, u32[]{:S(2)}) collective-permute-start(f32[114,128]{1,0:T(8,128)S(1)} %get-tuple-element.30), channel_id=1, source_target_pairs={{0,4},{1,5},{2,6},{3,7},{4,0},{5,1},{6,2},{7,3},{8,12},{9,13},{10,... | collective-permute-start | bytes 175112 | tf_op jit(solution)/shard_map/ppermute | solution.py:421
  10.9 3.1 %collective-permute-start.7 = (f32[114,128]{1,0:T(8,128)S(1)}, f32[114,128]{1,0:T(8,128)S(1)}, u32[]{:S(2)}, u32[]{:S(2)}) collective-permute-start(f32[114,128]{1,0:T(8,128)S(1)} %get-tuple-element.31), channel_id=1, source_target_pairs={{0,2},{1,3},{2,0},{3,1},{4,8},{5,9},{6,10},{7,11},{8,4},{9,5},{10,... | collective-permute-start | bytes 175112 | tf_op jit(solution)/shard_map/ppermute | solution.py:421
  13.9 0.0 collective-permute-done.4.za_ref
  14.0 0.0 collective-permute-done.5.zb_ref
  14.0 0.0 collective-permute-done.6.ca_ref
  14.0 2.2 %collective-permute-done.7.cb_ref = f32[114,128]{1,0:T(8,128)S(1)} collective-permute-done((f32[114,128]{1,0:T(8,128)S(1)}, f32[114,128]{1,0:T(8,128)S(1)}, u32[]{:S(2)}, u32[]{:S(2)}) %collective-permute-start.7) | collective-permute-done | bytes 58400 | tf_op jit(solution)/shard_map/ppermute | solution.py:421
  16.2 1.7 %finish.1 = (f32[512,128]{1,0:T(8,128)}, f32[32,128]{1,0:T(8,128)}) custom-call(f32[544,128]{1,0:T(8,128)S(1)} %get-tuple-element.21.src_ref, f32[112,128]{1,0:T(8,128)S(1)} %collective-permute-done.ya_ref, f32[112,128]{1,0:T(8,128)S(1)} %collective-permute-done.1.yb_ref, f32[424,128]{1,0:T(8,128)S(1)} %collective-permute-done.2.xa_ref, ...), custom_call_target="tpu_custom_call" | custom-call | tf_op jit(solution)/shard_map/finish/pallas_call | solution.py:490
  (2 shorter events, 0.1 us)
Async XLA Ops:
  3.0 7.3 %collective-permute-start.2 = (f32[424,128]{1,0:T(8,128)S(1)}, f32[424,128]{1,0:T(8,128)S(1)}, u32[]{:S(2)}, u32[]{:S(2)}) collective-permute-start(f32[424,128]{1,0:T(8,128)S(1)} %get-tuple-element.24), channel_id=1, source_target_pairs={{0,4},{1,5},{2,6},{3,7},{4,0},{5,1},{6,2},{7,3},{8,12},{9,13},{10,... | collective-permute-start | bytes 651272 | tf_op jit(solution)/shard_map/ppermute | solution.py:421
  3.5 6.8 %collective-permute-start.3 = (f32[424,128]{1,0:T(8,128)S(1)}, f32[424,128]{1,0:T(8,128)S(1)}, u32[]{:S(2)}, u32[]{:S(2)}) collective-permute-start(f32[424,128]{1,0:T(8,128)S(1)} %get-tuple-element.25), channel_id=1, source_target_pairs={{0,2},{1,3},{2,0},{3,1},{4,8},{5,9},{6,10},{7,11},{8,4},{9,5},{10,... | collective-permute-start | bytes 651272 | tf_op jit(solution)/shard_map/ppermute | solution.py:421
  6.1 4.2 %collective-permute-start = (f32[112,128]{1,0:T(8,128)S(1)}, f32[112,128]{1,0:T(8,128)S(1)}, u32[]{:S(2)}, u32[]{:S(2)}) collective-permute-start(f32[112,128]{1,0:T(8,128)S(1)} %get-tuple-element.22), channel_id=1, source_target_pairs={{0,1},{1,0},{2,3},{3,2},{4,5},{5,4},{6,7},{7,6},{8,9},{9,8},{10,11... | collective-permute-start | bytes 172040 | tf_op jit(solution)/shard_map/ppermute | solution.py:421
  7.6 2.7 %collective-permute-start.1 = (f32[112,128]{1,0:T(8,128)S(1)}, f32[112,128]{1,0:T(8,128)S(1)}, u32[]{:S(2)}, u32[]{:S(2)}) collective-permute-start(f32[112,128]{1,0:T(8,128)S(1)} %get-tuple-element.23), channel_id=1, source_target_pairs={{0,4},{1,2},{2,1},{3,7},{4,0},{5,6},{6,5},{7,3},{8,12},{9,10},{10,... | collective-permute-start | bytes 172040 | tf_op jit(solution)/shard_map/ppermute | solution.py:421
  7.6 6.4 %collective-permute-start.4 = (f32[114,128]{1,0:T(8,128)S(1)}, f32[114,128]{1,0:T(8,128)S(1)}, u32[]{:S(2)}, u32[]{:S(2)}) collective-permute-start(f32[114,128]{1,0:T(8,128)S(1)} %get-tuple-element.26), channel_id=1, source_target_pairs={{0,1},{1,0},{2,3},{3,2},{4,5},{5,4},{6,7},{7,6},{8,9},{9,8},{10,11... | collective-permute-start | bytes 175112 | tf_op jit(solution)/shard_map/ppermute | solution.py:421
  10.3 3.7 %collective-permute-start.5 = (f32[114,128]{1,0:T(8,128)S(1)}, f32[114,128]{1,0:T(8,128)S(1)}, u32[]{:S(2)}, u32[]{:S(2)}) collective-permute-start(f32[114,128]{1,0:T(8,128)S(1)} %get-tuple-element.27), channel_id=1, source_target_pairs={{0,4},{1,2},{2,1},{3,7},{4,0},{5,6},{6,5},{7,3},{8,12},{9,10},{10,... | collective-permute-start | bytes 175112 | tf_op jit(solution)/shard_map/ppermute | solution.py:421
  10.3 3.7 %collective-permute-start.6 = (f32[114,128]{1,0:T(8,128)S(1)}, f32[114,128]{1,0:T(8,128)S(1)}, u32[]{:S(2)}, u32[]{:S(2)}) collective-permute-start(f32[114,128]{1,0:T(8,128)S(1)} %get-tuple-element.30), channel_id=1, source_target_pairs={{0,4},{1,5},{2,6},{3,7},{4,0},{5,1},{6,2},{7,3},{8,12},{9,13},{10,... | collective-permute-start | bytes 175112 | tf_op jit(solution)/shard_map/ppermute | solution.py:421
  10.9 5.3 %collective-permute-start.7 = (f32[114,128]{1,0:T(8,128)S(1)}, f32[114,128]{1,0:T(8,128)S(1)}, u32[]{:S(2)}, u32[]{:S(2)}) collective-permute-start(f32[114,128]{1,0:T(8,128)S(1)} %get-tuple-element.31), channel_id=1, source_target_pairs={{0,2},{1,3},{2,0},{3,1},{4,8},{5,9},{6,10},{7,11},{8,4},{9,5},{10,... | collective-permute-start | bytes 175112 | tf_op jit(solution)/shard_map/ppermute | solution.py:421
where the time goes:
time: 18 us; the launch traced here: 17.8 us
  starting transfers between devices  10.2 us (57%)
  Pallas kernels  4.05 us (22%)
  waiting for transfers between devices  2.89 us (16%)
  between operations  0.68 us (4%)
    ppermute x8, starting transfers between devices, swap(): return lax.ppermute(value, ('gx', 'gy'), pairs)  10.2 us
    ppermute x8, waiting for transfers between devices, swap(): return lax.ppermute(value, ('gx', 'gy'), pairs)  2.89 us
    pallas_call x1, Pallas kernels, body(): pl.pallas_call(sources_kernel, name='sources', out_shape=[buffer(COMP * c...  2.33 us
    pallas_call x1, Pallas kernels, body(): pl.pallas_call(finish_kernel, name='finish', out_shape=[jax.ShapeDtypeStr...  1.66 us
  transfers between devices with their start and end apart: 8, of which 2 were waited for; matrix products, arithmetic and copies ran while one was open for 0% of the time, Pallas kernels for 0%

commit v1 on v0

--- a/solution.py
+++ b/solution.py
@@ -13,7 +13,7 @@
 BX = 4
 BY = 8
 NZ = 128
-CHUNKS = 4
+CHUNKS = 8
 GROUP = 4
 YROWS = 112
 ZROWS = 114

time: 18 us -> 17.9 us (level)
  no operation moved by 1% of the time
where the time goes in v1:
time: 17.9 us; the launch traced here: 17.8 us
  starting transfers between devices  10.2 us (57%)
  Pallas kernels  4.02 us (22%)
  waiting for transfers between devices  2.89 us (16%)
  between operations  0.68 us (4%)
    ppermute x8, starting transfers between devices, swap(): return lax.ppermute(value, ('gx', 'gy'), pairs)  10.2 us
    ppermute x8, waiting for transfers between devices, swap(): return lax.ppermute(value, ('gx', 'gy'), pairs)  2.89 us
    pallas_call x1, Pallas kernels, body(): pl.pallas_call(sources_kernel, name='sources', out_shape=[buffer(COMP * c...  2.3 us
    pallas_call x1, Pallas kernels, body(): pl.pallas_call(finish_kernel, name='finish', out_shape=[jax.ShapeDtypeStr...  1.66 us
  transfers between devices with their start and end apart: 8, of which 2 were waited for; matrix products, arithmetic and copies ran while one was open for 0% of the time, Pallas kernels for 0%

profile of v1, /device:TPU:0, one launch (start us, length us, event | category | flops | bytes accessed | tf_op | source)
XLA Modules:
  0.0 17.8 jit_solution(5676960421386993178)
XLA Ops:
  0.6 2.3 %sources.1 = (f32[544,128]{1,0:T(8,128)S(1)}, f32[112,128]{1,0:T(8,128)S(1)}, f32[112,128]{1,0:T(8,128)S(1)}, f32[424,128]{1,0:T(8,128)S(1)}, f32[424,128]{1,0:T...) custom-call(bf16[256,32,128]{2,1,0:T(8,128)(2,1)} %bitcast.11, ...), custom_call_target="tpu_custom_call" | custom-call | tf_op jit(solution)/shard_map/sources/pallas_call | solution.py:439
  2.9 0.5 %collective-permute-start.2 = (f32[424,128]{1,0:T(8,128)S(1)}, f32[424,128]{1,0:T(8,128)S(1)}, u32[]{:S(2)}, u32[]{:S(2)}) collective-permute-start(f32[424,128]{1,0:T(8,128)S(1)} %get-tuple-element.24), channel_id=1, source_target_pairs={{0,4},{1,5},{2,6},{3,7},{4,0},{5,1},{6,2},{7,3},{8,12},{9,13},{10,... | collective-permute-start | bytes 651272 | tf_op jit(solution)/shard_map/ppermute | solution.py:421
  3.4 2.6 %collective-permute-start.3 = (f32[424,128]{1,0:T(8,128)S(1)}, f32[424,128]{1,0:T(8,128)S(1)}, u32[]{:S(2)}, u32[]{:S(2)}) collective-permute-start(f32[424,128]{1,0:T(8,128)S(1)} %get-tuple-element.25), channel_id=1, source_target_pairs={{0,2},{1,3},{2,0},{3,1},{4,8},{5,9},{6,10},{7,11},{8,4},{9,5},{10,... | collective-permute-start | bytes 651272 | tf_op jit(solution)/shard_map/ppermute | solution.py:421
  6.0 1.5 %collective-permute-start = (f32[112,128]{1,0:T(8,128)S(1)}, f32[112,128]{1,0:T(8,128)S(1)}, u32[]{:S(2)}, u32[]{:S(2)}) collective-permute-start(f32[112,128]{1,0:T(8,128)S(1)} %get-tuple-element.22), channel_id=1, source_target_pairs={{0,1},{1,0},{2,3},{3,2},{4,5},{5,4},{6,7},{7,6},{8,9},{9,8},{10,11... | collective-permute-start | bytes 172040 | tf_op jit(solution)/shard_map/ppermute | solution.py:421
  7.5 0.0 collective-permute-start.1
  7.5 2.0 %collective-permute-start.4 = (f32[114,128]{1,0:T(8,128)S(1)}, f32[114,128]{1,0:T(8,128)S(1)}, u32[]{:S(2)}, u32[]{:S(2)}) collective-permute-start(f32[114,128]{1,0:T(8,128)S(1)} %get-tuple-element.26), channel_id=1, source_target_pairs={{0,1},{1,0},{2,3},{3,2},{4,5},{5,4},{6,7},{7,6},{8,9},{9,8},{10,11... | collective-permute-start | bytes 175112 | tf_op jit(solution)/shard_map/ppermute | solution.py:421
  9.5 0.7 %collective-permute-done.ya_ref = f32[112,128]{1,0:T(8,128)S(1)} collective-permute-done((f32[112,128]{1,0:T(8,128)S(1)}, f32[112,128]{1,0:T(8,128)S(1)}, u32[]{:S(2)}, u32[]{:S(2)}) %collective-permute-start) | collective-permute-done | bytes 57376 | tf_op jit(solution)/shard_map/ppermute | solution.py:421
  10.2 0.0 collective-permute-start.5
  10.2 0.0 collective-permute-done.1.yb_ref
  10.2 0.0 collective-permute-done.2.xa_ref
  10.2 0.0 collective-permute-done.3.xb_ref
  10.3 0.6 %collective-permute-start.6 = (f32[114,128]{1,0:T(8,128)S(1)}, f32[114,128]{1,0:T(8,128)S(1)}, u32[]{:S(2)}, u32[]{:S(2)}) collective-permute-start(f32[114,128]{1,0:T(8,128)S(1)} %get-tuple-element.30), channel_id=1, source_target_pairs={{0,4},{1,5},{2,6},{3,7},{4,0},{5,1},{6,2},{7,3},{8,12},{9,13},{10,... | collective-permute-start | bytes 175112 | tf_op jit(solution)/shard_map/ppermute | solution.py:421
  10.9 3.1 %collective-permute-start.7 = (f32[114,128]{1,0:T(8,128)S(1)}, f32[114,128]{1,0:T(8,128)S(1)}, u32[]{:S(2)}, u32[]{:S(2)}) collective-permute-start(f32[114,128]{1,0:T(8,128)S(1)} %get-tuple-element.31), channel_id=1, source_target_pairs={{0,2},{1,3},{2,0},{3,1},{4,8},{5,9},{6,10},{7,11},{8,4},{9,5},{10,... | collective-permute-start | bytes 175112 | tf_op jit(solution)/shard_map/ppermute | solution.py:421
  13.9 0.0 collective-permute-done.4.za_ref
  13.9 0.0 collective-permute-done.5.zb_ref
  13.9 0.0 collective-permute-done.6.ca_ref
  14.0 2.2 %collective-permute-done.7.cb_ref = f32[114,128]{1,0:T(8,128)S(1)} collective-permute-done((f32[114,128]{1,0:T(8,128)S(1)}, f32[114,128]{1,0:T(8,128)S(1)}, u32[]{:S(2)}, u32[]{:S(2)}) %collective-permute-start.7) | collective-permute-done | bytes 58400 | tf_op jit(solution)/shard_map/ppermute | solution.py:421
  16.1 1.7 %finish.1 = (f32[512,128]{1,0:T(8,128)}, f32[32,128]{1,0:T(8,128)}) custom-call(f32[544,128]{1,0:T(8,128)S(1)} %get-tuple-element.21.src_ref, f32[112,128]{1,0:T(8,128)S(1)} %collective-permute-done.ya_ref, f32[112,128]{1,0:T(8,128)S(1)} %collective-permute-done.1.yb_ref, f32[424,128]{1,0:T(8,128)S(1)} %collective-permute-done.2.xa_ref, ...), custom_call_target="tpu_custom_call" | custom-call | tf_op jit(solution)/shard_map/finish/pallas_call | solution.py:490
  (2 shorter events, 0.1 us)
Async XLA Ops:
  2.9 7.3 %collective-permute-start.2 = (f32[424,128]{1,0:T(8,128)S(1)}, f32[424,128]{1,0:T(8,128)S(1)}, u32[]{:S(2)}, u32[]{:S(2)}) collective-permute-start(f32[424,128]{1,0:T(8,128)S(1)} %get-tuple-element.24), channel_id=1, source_target_pairs={{0,4},{1,5},{2,6},{3,7},{4,0},{5,1},{6,2},{7,3},{8,12},{9,13},{10,... | collective-permute-start | bytes 651272 | tf_op jit(solution)/shard_map/ppermute | solution.py:421
  3.4 6.8 %collective-permute-start.3 = (f32[424,128]{1,0:T(8,128)S(1)}, f32[424,128]{1,0:T(8,128)S(1)}, u32[]{:S(2)}, u32[]{:S(2)}) collective-permute-start(f32[424,128]{1,0:T(8,128)S(1)} %get-tuple-element.25), channel_id=1, source_target_pairs={{0,2},{1,3},{2,0},{3,1},{4,8},{5,9},{6,10},{7,11},{8,4},{9,5},{10,... | collective-permute-start | bytes 651272 | tf_op jit(solution)/shard_map/ppermute | solution.py:421
  6.0 4.2 %collective-permute-start = (f32[112,128]{1,0:T(8,128)S(1)}, f32[112,128]{1,0:T(8,128)S(1)}, u32[]{:S(2)}, u32[]{:S(2)}) collective-permute-start(f32[112,128]{1,0:T(8,128)S(1)} %get-tuple-element.22), channel_id=1, source_target_pairs={{0,1},{1,0},{2,3},{3,2},{4,5},{5,4},{6,7},{7,6},{8,9},{9,8},{10,11... | collective-permute-start | bytes 172040 | tf_op jit(solution)/shard_map/ppermute | solution.py:421
  7.5 2.7 %collective-permute-start.1 = (f32[112,128]{1,0:T(8,128)S(1)}, f32[112,128]{1,0:T(8,128)S(1)}, u32[]{:S(2)}, u32[]{:S(2)}) collective-permute-start(f32[112,128]{1,0:T(8,128)S(1)} %get-tuple-element.23), channel_id=1, source_target_pairs={{0,4},{1,2},{2,1},{3,7},{4,0},{5,6},{6,5},{7,3},{8,12},{9,10},{10,... | collective-permute-start | bytes 172040 | tf_op jit(solution)/shard_map/ppermute | solution.py:421
  7.5 6.4 %collective-permute-start.4 = (f32[114,128]{1,0:T(8,128)S(1)}, f32[114,128]{1,0:T(8,128)S(1)}, u32[]{:S(2)}, u32[]{:S(2)}) collective-permute-start(f32[114,128]{1,0:T(8,128)S(1)} %get-tuple-element.26), channel_id=1, source_target_pairs={{0,1},{1,0},{2,3},{3,2},{4,5},{5,4},{6,7},{7,6},{8,9},{9,8},{10,11... | collective-permute-start | bytes 175112 | tf_op jit(solution)/shard_map/ppermute | solution.py:421
  10.2 3.7 %collective-permute-start.5 = (f32[114,128]{1,0:T(8,128)S(1)}, f32[114,128]{1,0:T(8,128)S(1)}, u32[]{:S(2)}, u32[]{:S(2)}) collective-permute-start(f32[114,128]{1,0:T(8,128)S(1)} %get-tuple-element.27), channel_id=1, source_target_pairs={{0,4},{1,2},{2,1},{3,7},{4,0},{5,6},{6,5},{7,3},{8,12},{9,10},{10,... | collective-permute-start | bytes 175112 | tf_op jit(solution)/shard_map/ppermute | solution.py:421
  10.3 3.7 %collective-permute-start.6 = (f32[114,128]{1,0:T(8,128)S(1)}, f32[114,128]{1,0:T(8,128)S(1)}, u32[]{:S(2)}, u32[]{:S(2)}) collective-permute-start(f32[114,128]{1,0:T(8,128)S(1)} %get-tuple-element.30), channel_id=1, source_target_pairs={{0,4},{1,5},{2,6},{3,7},{4,0},{5,1},{6,2},{7,3},{8,12},{9,13},{10,... | collective-permute-start | bytes 175112 | tf_op jit(solution)/shard_map/ppermute | solution.py:421
  10.9 5.3 %collective-permute-start.7 = (f32[114,128]{1,0:T(8,128)S(1)}, f32[114,128]{1,0:T(8,128)S(1)}, u32[]{:S(2)}, u32[]{:S(2)}) collective-permute-start(f32[114,128]{1,0:T(8,128)S(1)} %get-tuple-element.31), channel_id=1, source_target_pairs={{0,2},{1,3},{2,0},{3,1},{4,8},{5,9},{6,10},{7,11},{8,4},{9,5},{10,... | collective-permute-start | bytes 175112 | tf_op jit(solution)/shard_map/ppermute | solution.py:421

commit v2 on v1

--- a/solution.py
+++ b/solution.py
@@ -1,3 +1,5 @@
+import functools
+
 import jax
 import jax.numpy as jnp
 from jax import lax
@@ -182,39 +184,16 @@
     clear(cb_ref, alone_b)
 
 
-def sort_kernel(za_ref, zb_ref, zlow_ref, zhigh_ref):
-    a_is_high = place("gy")[0] == 1
-    a = za_ref[...]
-    b = zb_ref[...]
-    zlow_ref[...] = jnp.where(a_is_high, b, a)
-    zhigh_ref[...] = jnp.where(a_is_high, a, b)
-
-
-def finish_kernel(
-    src_ref, ya_ref, yb_ref, xa_ref, xb_ref, zlow_ref, zhigh_ref, ca_ref, cb_ref,
-    dens_ref, metals_ref, energy_ref, cx_ref, cy_ref, cz_ref,
-    out_hbm, energy_out_hbm,
-    out_ref, energy_out_ref, sems,
-    se_ref, de_ref, rw_ref, ys_ref, ee_ref, mx_ref, my_ref, cxl_ref, cye_ref,
+def layout_kernel(
+    src_ref, ya_ref, yb_ref, xa_ref, xb_ref, za_ref, zb_ref, dens_ref, cy_ref,
+    se_ref, de_ref, mx_ref, my_ref, cxl_ref, cye_ref,
 ):
     even_x = place("gx")[0]
     even_y = place("gy")[0]
-    lane = lax.broadcasted_iota(jnp.int32, (1, NZ), 1)
-    not_first = lane > 0
-    not_last = lane < NZ - 1
-
-    def prev_z(v):
-        return pltpu.roll(v, 1, 1)
-
-    def next_z(v):
-        return pltpu.roll(v, NZ - 1, 1)
-
-    def masked_prev(v):
-        return jnp.where(not_first, prev_z(v), 0.0)
-
-    def masked_next(v):
-        return jnp.where(not_last, next_z(v), 0.0)
-
+    a = za_ref[...]
+    b = zb_ref[...]
+    low = jnp.where(even_y == 1, b, a)
+    high_part = jnp.where(even_y == 1, a, b)
     de_ref[...] = jnp.zeros(de_ref.shape, F32)
 
     for x in range(BX):
@@ -241,15 +220,15 @@
         for w in range(3):
             d_row = jnp.where(is_high, 24 + w, 15 - w)
             de_ref[rows(3 * DPITCH + d_row, BX, DPITCH), :] = y_ref[100 + 4 * w : 104 + 4 * w, :]
-    for side, z_ref in enumerate((zlow_ref, zhigh_ref)):
+    for side, part in enumerate((low, high_part)):
         for k in range(NMET):
-            my_ref[side, k * 8 + 2 : k * 8 + 2 + BX, :] = z_ref[k * BX : k * BX + BX, :]
+            my_ref[side, k * 8 + 2 : k * 8 + 2 + BX, :] = part[k * BX : k * BX + BX, :]
         for x in range(1, BX - 1):
             r2 = (6, 17)[side]
-            se_ref[rows((x + 2) * PITCH + r2, NMET, 8 * PITCH), :] = z_ref[48 + 16 * x : 64 + 16 * x, :]
-    cye_ref[rows(7, BX, PITCH), :] = zlow_ref[96:100, :]
-
-    for x_ref, c_ref, high in ((xa_ref, ca_ref, even_x), (xb_ref, cb_ref, 1 - even_x)):
+            se_ref[rows((x + 2) * PITCH + r2, NMET, 8 * PITCH), :] = part[48 + 16 * x : 64 + 16 * x, :]
+    cye_ref[rows(7, BX, PITCH), :] = low[96:100, :]
+
+    for x_ref, high in ((xa_ref, even_x), (xb_ref, 1 - even_x)):
         is_high = high == 1
         p1 = jnp.where(is_high, 6, 1)
         p2 = jnp.where(is_high, 7, 0)
@@ -269,6 +248,38 @@
             de_ref[pl.ds(at, BY), :] = x_ref[tile * BY : tile * BY + BY, :]
         tile = COMP + 2 * NMET + 3
         cxl_ref[high] = x_ref[tile * BY : tile * BY + BY, :]
+
+
+def finish_kernel(
+    se_in_ref, de_in_ref, mx_ref, my_ref, cxl_ref, cye_ref, ca_ref, cb_ref,
+    metals_ref, energy_ref, cx_ref, cy_ref, cz_ref,
+    out_hbm, energy_out_hbm, se_ref, de_ref,
+    out_ref, energy_out_ref, sems,
+    rw_ref, ys_ref, ee_ref,
+):
+    del se_in_ref, de_in_ref
+    even_x = place("gx")[0]
+    even_y = place("gy")[0]
+    lane = lax.broadcasted_iota(jnp.int32, (1, NZ), 1)
+    not_first = lane > 0
+    not_last = lane < NZ - 1
+
+    def prev_z(v):
+        return pltpu.roll(v, 1, 1)
+
+    def next_z(v):
+        return pltpu.roll(v, NZ - 1, 1)
+
+    def masked_prev(v):
+        return jnp.where(not_first, prev_z(v), 0.0)
+
+    def masked_next(v):
+        return jnp.where(not_last, next_z(v), 0.0)
+
+    for c_ref, high in ((ca_ref, even_x), (cb_ref, 1 - even_x)):
+        is_high = high == 1
+        p1 = jnp.where(is_high, 6, 1)
+        p2 = jnp.where(is_high, 7, 0)
         for side, y_high in enumerate((even_y, 1 - even_y)):
             base = 48 * side
             y_is_high = y_high == 1
@@ -479,44 +490,48 @@
     )(*(pltpu.with_memory_space_constraint(a, pltpu.VMEM) for a in (ya, yb, xa, xb)))
     ca = swap(ca, pairs_xa)
     cb = swap(cb, pairs_xb)
-    z = pl.pallas_call(
-        sort_kernel,
-        name="sort",
-        out_shape=[buffer(ZROWS), buffer(ZROWS)],
-        in_specs=[VM] * 2,
-        out_specs=[VM] * 2,
-        compiler_params=pltpu.CompilerParams(vmem_limit_bytes=4 * 1024 * 1024),
-    )(*(pltpu.with_memory_space_constraint(a, pltpu.VMEM) for a in (za, zb)))
-    advected, energy_out = pl.pallas_call(
+    dens, metals, energy, cx, cy, cz = local
+    in_vmem = functools.partial(pltpu.with_memory_space_constraint, memory_space=pltpu.VMEM)
+    shape_se, shape_de = buffer(COMP * 8 * PITCH), buffer(10 * DPITCH)
+    operands = [src, ya, yb, xa, xb, za, zb, dens, cy]
+    laid = pl.pallas_call(
+        layout_kernel,
+        name="layout",
+        out_shape=[
+            shape_se,
+            shape_de,
+            pltpu.VMEM((2, NMET * BY, NZ), F32),
+            pltpu.VMEM((2, NMET * 8, NZ), F32),
+            pltpu.VMEM((2, BY, NZ), F32),
+            buffer(BX * PITCH),
+        ],
+        in_specs=[VM] * len(operands),
+        out_specs=[VM] * 6,
+        compiler_params=pltpu.CompilerParams(vmem_limit_bytes=16 * 1024 * 1024),
+    )(*map(in_vmem, operands))
+    operands = [*laid, ca, cb, metals, energy, cx, cy, cz]
+    advected, energy_out, _, _ = pl.pallas_call(
         finish_kernel,
         name="finish",
         out_shape=[
             jax.ShapeDtypeStruct((NMET * cells, NZ), F32),
             jax.ShapeDtypeStruct((cells, NZ), F32),
+            shape_se,
+            shape_de,
         ],
-        in_specs=[VM] * 15,
-        out_specs=[HB, HB],
+        in_specs=[VM] * len(operands),
+        out_specs=[HB, HB, VM, VM],
+        input_output_aliases={0: 2, 1: 3},
         scratch_shapes=[
             pltpu.VMEM((NMET * cells, NZ), F32),
             pltpu.VMEM((cells, NZ), F32),
             pltpu.SemaphoreType.DMA((1 + NMET // GROUP,)),
-            pltpu.VMEM((COMP * 8 * PITCH, NZ), F32),
-            pltpu.VMEM((10 * DPITCH, NZ), F32),
             pltpu.VMEM((8 * PITCH, NZ), F32),
             pltpu.VMEM((COMP * 8 * BY, NZ), F32),
             pltpu.VMEM((NMET * 8 * PITCH, NZ), F32),
-            pltpu.VMEM((2, NMET * BY, NZ), F32),
-            pltpu.VMEM((2, NMET * 8, NZ), F32),
-            pltpu.VMEM((2, BY, NZ), F32),
-            pltpu.VMEM((BX * PITCH, NZ), F32),
         ],
         compiler_params=pltpu.CompilerParams(vmem_limit_bytes=32 * 1024 * 1024),
-    )(
-        *(
-            pltpu.with_memory_space_constraint(a, pltpu.VMEM)
-            for a in (src, ya, yb, xa, xb, *z, ca, cb, *local)
-        )
-    )
+    )(*map(in_vmem, operands))
     return advected.reshape(NMET, BX, BY, NZ), energy_out.reshape(BX, BY, NZ)
 
 

time: 17.9 us -> 17.8 us (level)
  transfers between devices with their start and end apart: 8 -> 8, of which waited for: 2 -> 2; matrix products, arithmetic and copies ran while one was open for 0% -> 0% of each run, Pallas kernels for 0% -> 1%
where the time goes in v2:
time: 17.8 us; the launch traced here: 17.6 us
  starting transfers between devices  10.2 us (57%)
  Pallas kernels  4.03 us (23%)
  waiting for transfers between devices  2.76 us (16%)
  between operations  0.68 us (4%)
    ppermute x8, starting transfers between devices, swap(): return lax.ppermute(value, ('gx', 'gy'), pairs)  10.2 us
    ppermute x8, waiting for transfers between devices, swap(): return lax.ppermute(value, ('gx', 'gy'), pairs)  2.76 us
    pallas_call x1, Pallas kernels, body(): pl.pallas_call(sources_kernel, name='sources', out_shape=[buffer(COMP * c...  2.3 us
    pallas_call x1, Pallas kernels, body(): pl.pallas_call(finish_kernel, name='finish', out_shape=[jax.ShapeDtypeStr...  1.53 us
  transfers between devices with their start and end apart: 8, of which 2 were waited for; matrix products, arithmetic and copies ran while one was open for 0% of the time, Pallas kernels for 1%

profile of v2, /device:TPU:0, one launch (start us, length us, event | category | flops | bytes accessed | tf_op | source)
XLA Modules:
  0.0 17.6 jit_solution(14598333075459839281)
XLA Ops:
  0.6 2.3 %sources.1 = (f32[544,128]{1,0:T(8,128)S(1)}, f32[112,128]{1,0:T(8,128)S(1)}, f32[112,128]{1,0:T(8,128)S(1)}, f32[424,128]{1,0:T(8,128)S(1)}, f32[424,128]{1,0:T...) custom-call(bf16[256,32,128]{2,1,0:T(8,128)(2,1)} %bitcast.11, ...), custom_call_target="tpu_custom_call" | custom-call | tf_op jit(solution)/shard_map/sources/pallas_call | solution.py:450
  2.9 0.5 %collective-permute-start.2 = (f32[424,128]{1,0:T(8,128)S(1)}, f32[424,128]{1,0:T(8,128)S(1)}, u32[]{:S(2)}, u32[]{:S(2)}) collective-permute-start(f32[424,128]{1,0:T(8,128)S(1)} %get-tuple-element.28), channel_id=1, source_target_pairs={{0,4},{1,5},{2,6},{3,7},{4,0},{5,1},{6,2},{7,3},{8,12},{9,13},{10,... | collective-permute-start | bytes 651272 | tf_op jit(solution)/shard_map/ppermute | solution.py:432
  3.4 2.6 %collective-permute-start.3 = (f32[424,128]{1,0:T(8,128)S(1)}, f32[424,128]{1,0:T(8,128)S(1)}, u32[]{:S(2)}, u32[]{:S(2)}) collective-permute-start(f32[424,128]{1,0:T(8,128)S(1)} %get-tuple-element.29), channel_id=1, source_target_pairs={{0,2},{1,3},{2,0},{3,1},{4,8},{5,9},{6,10},{7,11},{8,4},{9,5},{10,... | collective-permute-start | bytes 651272 | tf_op jit(solution)/shard_map/ppermute | solution.py:432
  6.0 1.5 %collective-permute-start = (f32[112,128]{1,0:T(8,128)S(1)}, f32[112,128]{1,0:T(8,128)S(1)}, u32[]{:S(2)}, u32[]{:S(2)}) collective-permute-start(f32[112,128]{1,0:T(8,128)S(1)} %get-tuple-element.26), channel_id=1, source_target_pairs={{0,1},{1,0},{2,3},{3,2},{4,5},{5,4},{6,7},{7,6},{8,9},{9,8},{10,11... | collective-permute-start | bytes 172040 | tf_op jit(solution)/shard_map/ppermute | solution.py:432
  7.5 0.0 collective-permute-start.1
  7.5 2.0 %collective-permute-start.4 = (f32[114,128]{1,0:T(8,128)S(1)}, f32[114,128]{1,0:T(8,128)S(1)}, u32[]{:S(2)}, u32[]{:S(2)}) collective-permute-start(f32[114,128]{1,0:T(8,128)S(1)} %get-tuple-element.30), channel_id=1, source_target_pairs={{0,1},{1,0},{2,3},{3,2},{4,5},{5,4},{6,7},{7,6},{8,9},{9,8},{10,11... | collective-permute-start | bytes 175112 | tf_op jit(solution)/shard_map/ppermute | solution.py:432
  9.5 0.7 %collective-permute-done.ya_ref = f32[112,128]{1,0:T(8,128)S(1)} collective-permute-done((f32[112,128]{1,0:T(8,128)S(1)}, f32[112,128]{1,0:T(8,128)S(1)}, u32[]{:S(2)}, u32[]{:S(2)}) %collective-permute-start) | collective-permute-done | bytes 57376 | tf_op jit(solution)/shard_map/ppermute | solution.py:432
  10.2 0.0 collective-permute-start.5
  10.2 0.0 collective-permute-done.1.yb_ref
  10.2 0.0 collective-permute-done.2.xa_ref
  10.2 0.0 collective-permute-done.3.xb_ref
  10.3 0.6 %collective-permute-start.6 = (f32[114,128]{1,0:T(8,128)S(1)}, f32[114,128]{1,0:T(8,128)S(1)}, u32[]{:S(2)}, u32[]{:S(2)}) collective-permute-start(f32[114,128]{1,0:T(8,128)S(1)} %get-tuple-element.40), channel_id=1, source_target_pairs={{0,4},{1,5},{2,6},{3,7},{4,0},{5,1},{6,2},{7,3},{8,12},{9,13},{10,... | collective-permute-start | bytes 175112 | tf_op jit(solution)/shard_map/ppermute | solution.py:432
  10.9 3.1 %collective-permute-start.7 = (f32[114,128]{1,0:T(8,128)S(1)}, f32[114,128]{1,0:T(8,128)S(1)}, u32[]{:S(2)}, u32[]{:S(2)}) collective-permute-start(f32[114,128]{1,0:T(8,128)S(1)} %get-tuple-element.41), channel_id=1, source_target_pairs={{0,2},{1,3},{2,0},{3,1},{4,8},{5,9},{6,10},{7,11},{8,4},{9,5},{10,... | collective-permute-start | bytes 175112 | tf_op jit(solution)/shard_map/ppermute | solution.py:432
  13.9 0.0 collective-permute-done.4.za_ref
  13.9 0.0 collective-permute-done.5.zb_ref
  13.9 0.2 layout.1
  14.1 0.0 collective-permute-done.6.ca_ref
  14.1 2.0 %collective-permute-done.7.cb_ref = f32[114,128]{1,0:T(8,128)S(1)} collective-permute-done((f32[114,128]{1,0:T(8,128)S(1)}, f32[114,128]{1,0:T(8,128)S(1)}, u32[]{:S(2)}, u32[]{:S(2)}) %collective-permute-start.7) | collective-permute-done | bytes 58400 | tf_op jit(solution)/shard_map/ppermute | solution.py:432
  16.1 1.5 %finish.1 = (f32[512,128]{1,0:T(8,128)}, f32[32,128]{1,0:T(8,128)}, f32[3264,128]{1,0:T(8,128)S(1)}, f32[400,128]{1,0:T(8,128)S(1)}) custom-call(f32[3264,128]{1,0:T(8,128)S(1)} %get-tuple-element.34.se_in_ref, f32[400,128]{1,0:T(8,128)S(1)} %get-tuple-element.35.de_in_ref, ...), custom_call_target="tpu_custom_call", output_to_operand_aliasing={{2}: (0, {}), {3}: (1, {})} | custom-call | tf_op jit(solution)/shard_map/finish/pallas_call | solution.py:513
  (1 shorter events, 0.0 us)
Async XLA Ops:
  2.9 7.3 %collective-permute-start.2 = (f32[424,128]{1,0:T(8,128)S(1)}, f32[424,128]{1,0:T(8,128)S(1)}, u32[]{:S(2)}, u32[]{:S(2)}) collective-permute-start(f32[424,128]{1,0:T(8,128)S(1)} %get-tuple-element.28), channel_id=1, source_target_pairs={{0,4},{1,5},{2,6},{3,7},{4,0},{5,1},{6,2},{7,3},{8,12},{9,13},{10,... | collective-permute-start | bytes 651272 | tf_op jit(solution)/shard_map/ppermute | solution.py:432
  3.4 6.8 %collective-permute-start.3 = (f32[424,128]{1,0:T(8,128)S(1)}, f32[424,128]{1,0:T(8,128)S(1)}, u32[]{:S(2)}, u32[]{:S(2)}) collective-permute-start(f32[424,128]{1,0:T(8,128)S(1)} %get-tuple-element.29), channel_id=1, source_target_pairs={{0,2},{1,3},{2,0},{3,1},{4,8},{5,9},{6,10},{7,11},{8,4},{9,5},{10,... | collective-permute-start | bytes 651272 | tf_op jit(solution)/shard_map/ppermute | solution.py:432
  6.0 4.2 %collective-permute-start = (f32[112,128]{1,0:T(8,128)S(1)}, f32[112,128]{1,0:T(8,128)S(1)}, u32[]{:S(2)}, u32[]{:S(2)}) collective-permute-start(f32[112,128]{1,0:T(8,128)S(1)} %get-tuple-element.26), channel_id=1, source_target_pairs={{0,1},{1,0},{2,3},{3,2},{4,5},{5,4},{6,7},{7,6},{8,9},{9,8},{10,11... | collective-permute-start | bytes 172040 | tf_op jit(solution)/shard_map/ppermute | solution.py:432
  7.5 2.7 %collective-permute-start.1 = (f32[112,128]{1,0:T(8,128)S(1)}, f32[112,128]{1,0:T(8,128)S(1)}, u32[]{:S(2)}, u32[]{:S(2)}) collective-permute-start(f32[112,128]{1,0:T(8,128)S(1)} %get-tuple-element.27), channel_id=1, source_target_pairs={{0,4},{1,2},{2,1},{3,7},{4,0},{5,6},{6,5},{7,3},{8,12},{9,10},{10,... | collective-permute-start | bytes 172040 | tf_op jit(solution)/shard_map/ppermute | solution.py:432
  7.5 6.4 %collective-permute-start.4 = (f32[114,128]{1,0:T(8,128)S(1)}, f32[114,128]{1,0:T(8,128)S(1)}, u32[]{:S(2)}, u32[]{:S(2)}) collective-permute-start(f32[114,128]{1,0:T(8,128)S(1)} %get-tuple-element.30), channel_id=1, source_target_pairs={{0,1},{1,0},{2,3},{3,2},{4,5},{5,4},{6,7},{7,6},{8,9},{9,8},{10,11... | collective-permute-start | bytes 175112 | tf_op jit(solution)/shard_map/ppermute | solution.py:432
  10.2 3.7 %collective-permute-start.5 = (f32[114,128]{1,0:T(8,128)S(1)}, f32[114,128]{1,0:T(8,128)S(1)}, u32[]{:S(2)}, u32[]{:S(2)}) collective-permute-start(f32[114,128]{1,0:T(8,128)S(1)} %get-tuple-element.31), channel_id=1, source_target_pairs={{0,4},{1,2},{2,1},{3,7},{4,0},{5,6},{6,5},{7,3},{8,12},{9,10},{10,... | collective-permute-start | bytes 175112 | tf_op jit(solution)/shard_map/ppermute | solution.py:432
  10.3 3.8 %collective-permute-start.6 = (f32[114,128]{1,0:T(8,128)S(1)}, f32[114,128]{1,0:T(8,128)S(1)}, u32[]{:S(2)}, u32[]{:S(2)}) collective-permute-start(f32[114,128]{1,0:T(8,128)S(1)} %get-tuple-element.40), channel_id=1, source_target_pairs={{0,4},{1,5},{2,6},{3,7},{4,0},{5,1},{6,2},{7,3},{8,12},{9,13},{10,... | collective-permute-start | bytes 175112 | tf_op jit(solution)/shard_map/ppermute | solution.py:432
  10.9 5.3 %collective-permute-start.7 = (f32[114,128]{1,0:T(8,128)S(1)}, f32[114,128]{1,0:T(8,128)S(1)}, u32[]{:S(2)}, u32[]{:S(2)}) collective-permute-start(f32[114,128]{1,0:T(8,128)S(1)} %get-tuple-element.41), channel_id=1, source_target_pairs={{0,2},{1,3},{2,0},{3,1},{4,8},{5,9},{6,10},{7,11},{8,4},{9,5},{10,... | collective-permute-start | bytes 175112 | tf_op jit(solution)/shard_map/ppermute | solution.py:432

commit v3 on v2

--- a/solution.py
+++ b/solution.py
@@ -50,7 +50,10 @@
         (cx_hbm, cx_ref), (cy_hbm, cy_ref), (cz_hbm, cz_ref), (energy_hbm, energy_ref),
     ]
     small_copies = [
-        pltpu.make_async_copy(hbm, ref, sems.at[i]) for i, (hbm, ref) in enumerate(small)
+        pltpu.make_async_copy(
+            hbm, ref if i < 2 else ref.at[pl.ds(0, hbm.shape[0])], sems.at[i]
+        )
+        for i, (hbm, ref) in enumerate(small)
     ]
     per = BINS // CHUNKS
     copies = [
@@ -450,9 +453,9 @@
     src, ya, yb, xa, xb, za, zb, *local = pl.pallas_call(
         sources_kernel,
         name="sources",
-        out_shape=[buffer(COMP * cells)]
+        out_shape=[buffer(COMP * cells + BY)]
         + [buffer(count) for count in (YROWS, YROWS, XROWS, XROWS, ZROWS, ZROWS)]
-        + [buffer(cells), buffer(NMET * cells)] + [buffer(cells)] * 4,
+        + [buffer(cells + BY), buffer(NMET * cells + BY)] + [buffer(cells + BY)] * 4,
         in_specs=[HB] * 9,
         out_specs=[VM] * 13,
         scratch_shapes=[

time: 17.8 us -> 17.8 us (level)
  no operation moved by 1% of the time
where the time goes in v3:
time: 17.8 us; the launch traced here: 17.7 us
  starting transfers between devices  10.2 us (57%)
  Pallas kernels  4.06 us (23%)
  waiting for transfers between devices  2.75 us (15%)
  between operations  0.68 us (4%)
    ppermute x8, starting transfers between devices, swap(): return lax.ppermute(value, ('gx', 'gy'), pairs)  10.2 us
    ppermute x8, waiting for transfers between devices, swap(): return lax.ppermute(value, ('gx', 'gy'), pairs)  2.75 us
    pallas_call x1, Pallas kernels, body(): pl.pallas_call(sources_kernel, name='sources', out_shape=[buffer(COMP * c...  2.3 us
    pallas_call x1, Pallas kernels, body(): pl.pallas_call(finish_kernel, name='finish', out_shape=[jax.ShapeDtypeStr...  1.56 us
  transfers between devices with their start and end apart: 8, of which 2 were waited for; matrix products, arithmetic and copies ran while one was open for 0% of the time, Pallas kernels for 1%

profile of v3, /device:TPU:0, one launch (start us, length us, event | category | flops | bytes accessed | tf_op | source)
XLA Modules:
  0.0 17.7 jit_solution(210121363024777733)
XLA Ops:
  0.6 2.3 %sources.1 = (f32[552,128]{1,0:T(8,128)S(1)}, f32[112,128]{1,0:T(8,128)S(1)}, f32[112,128]{1,0:T(8,128)S(1)}, f32[424,128]{1,0:T(8,128)S(1)}, f32[424,128]{1,0:T...) custom-call(bf16[256,32,128]{2,1,0:T(8,128)(2,1)} %bitcast.11, ...), custom_call_target="tpu_custom_call" | custom-call | tf_op jit(solution)/shard_map/sources/pallas_call | solution.py:453
  2.9 0.5 %collective-permute-start.2 = (f32[424,128]{1,0:T(8,128)S(1)}, f32[424,128]{1,0:T(8,128)S(1)}, u32[]{:S(2)}, u32[]{:S(2)}) collective-permute-start(f32[424,128]{1,0:T(8,128)S(1)} %get-tuple-element.28), channel_id=1, source_target_pairs={{0,4},{1,5},{2,6},{3,7},{4,0},{5,1},{6,2},{7,3},{8,12},{9,13},{10,... | collective-permute-start | bytes 651272 | tf_op jit(solution)/shard_map/ppermute | solution.py:435
  3.4 2.6 %collective-permute-start.3 = (f32[424,128]{1,0:T(8,128)S(1)}, f32[424,128]{1,0:T(8,128)S(1)}, u32[]{:S(2)}, u32[]{:S(2)}) collective-permute-start(f32[424,128]{1,0:T(8,128)S(1)} %get-tuple-element.29), channel_id=1, source_target_pairs={{0,2},{1,3},{2,0},{3,1},{4,8},{5,9},{6,10},{7,11},{8,4},{9,5},{10,... | collective-permute-start | bytes 651272 | tf_op jit(solution)/shard_map/ppermute | solution.py:435
  6.0 1.5 %collective-permute-start = (f32[112,128]{1,0:T(8,128)S(1)}, f32[112,128]{1,0:T(8,128)S(1)}, u32[]{:S(2)}, u32[]{:S(2)}) collective-permute-start(f32[112,128]{1,0:T(8,128)S(1)} %get-tuple-element.26), channel_id=1, source_target_pairs={{0,1},{1,0},{2,3},{3,2},{4,5},{5,4},{6,7},{7,6},{8,9},{9,8},{10,11... | collective-permute-start | bytes 172040 | tf_op jit(solution)/shard_map/ppermute | solution.py:435
  7.5 0.0 collective-permute-start.1
  7.5 2.0 %collective-permute-start.4 = (f32[114,128]{1,0:T(8,128)S(1)}, f32[114,128]{1,0:T(8,128)S(1)}, u32[]{:S(2)}, u32[]{:S(2)}) collective-permute-start(f32[114,128]{1,0:T(8,128)S(1)} %get-tuple-element.30), channel_id=1, source_target_pairs={{0,1},{1,0},{2,3},{3,2},{4,5},{5,4},{6,7},{7,6},{8,9},{9,8},{10,11... | collective-permute-start | bytes 175112 | tf_op jit(solution)/shard_map/ppermute | solution.py:435
  9.5 0.7 %collective-permute-done.ya_ref = f32[112,128]{1,0:T(8,128)S(1)} collective-permute-done((f32[112,128]{1,0:T(8,128)S(1)}, f32[112,128]{1,0:T(8,128)S(1)}, u32[]{:S(2)}, u32[]{:S(2)}) %collective-permute-start) | collective-permute-done | bytes 57376 | tf_op jit(solution)/shard_map/ppermute | solution.py:435
  10.2 0.0 collective-permute-start.5
  10.2 0.0 collective-permute-done.1.yb_ref
  10.2 0.0 collective-permute-done.2.xa_ref
  10.2 0.0 collective-permute-done.3.xb_ref
  10.3 0.6 %collective-permute-start.6 = (f32[114,128]{1,0:T(8,128)S(1)}, f32[114,128]{1,0:T(8,128)S(1)}, u32[]{:S(2)}, u32[]{:S(2)}) collective-permute-start(f32[114,128]{1,0:T(8,128)S(1)} %get-tuple-element.40), channel_id=1, source_target_pairs={{0,4},{1,5},{2,6},{3,7},{4,0},{5,1},{6,2},{7,3},{8,12},{9,13},{10,... | collective-permute-start | bytes 175112 | tf_op jit(solution)/shard_map/ppermute | solution.py:435
  10.9 3.0 %collective-permute-start.7 = (f32[114,128]{1,0:T(8,128)S(1)}, f32[114,128]{1,0:T(8,128)S(1)}, u32[]{:S(2)}, u32[]{:S(2)}) collective-permute-start(f32[114,128]{1,0:T(8,128)S(1)} %get-tuple-element.41), channel_id=1, source_target_pairs={{0,2},{1,3},{2,0},{3,1},{4,8},{5,9},{6,10},{7,11},{8,4},{9,5},{10,... | collective-permute-start | bytes 175112 | tf_op jit(solution)/shard_map/ppermute | solution.py:435
  13.9 0.0 collective-permute-done.4.za_ref
  13.9 0.0 collective-permute-done.5.zb_ref
  13.9 0.2 layout.1
  14.1 0.0 collective-permute-done.6.ca_ref
  14.1 2.0 %collective-permute-done.7.cb_ref = f32[114,128]{1,0:T(8,128)S(1)} collective-permute-done((f32[114,128]{1,0:T(8,128)S(1)}, f32[114,128]{1,0:T(8,128)S(1)}, u32[]{:S(2)}, u32[]{:S(2)}) %collective-permute-start.7) | collective-permute-done | bytes 58400 | tf_op jit(solution)/shard_map/ppermute | solution.py:435
  16.1 1.6 %finish.1 = (f32[512,128]{1,0:T(8,128)}, f32[32,128]{1,0:T(8,128)}, f32[3264,128]{1,0:T(8,128)S(1)}, f32[400,128]{1,0:T(8,128)S(1)}) custom-call(f32[3264,128]{1,0:T(8,128)S(1)} %get-tuple-element.34.se_in_ref, f32[400,128]{1,0:T(8,128)S(1)} %get-tuple-element.35.de_in_ref, ...), custom_call_target="tpu_custom_call", output_to_operand_aliasing={{2}: (0, {}), {3}: (1, {})} | custom-call | tf_op jit(solution)/shard_map/finish/pallas_call | solution.py:516
  (1 shorter events, 0.0 us)
Async XLA Ops:
  2.9 7.3 %collective-permute-start.2 = (f32[424,128]{1,0:T(8,128)S(1)}, f32[424,128]{1,0:T(8,128)S(1)}, u32[]{:S(2)}, u32[]{:S(2)}) collective-permute-start(f32[424,128]{1,0:T(8,128)S(1)} %get-tuple-element.28), channel_id=1, source_target_pairs={{0,4},{1,5},{2,6},{3,7},{4,0},{5,1},{6,2},{7,3},{8,12},{9,13},{10,... | collective-permute-start | bytes 651272 | tf_op jit(solution)/shard_map/ppermute | solution.py:435
  3.4 6.8 %collective-permute-start.3 = (f32[424,128]{1,0:T(8,128)S(1)}, f32[424,128]{1,0:T(8,128)S(1)}, u32[]{:S(2)}, u32[]{:S(2)}) collective-permute-start(f32[424,128]{1,0:T(8,128)S(1)} %get-tuple-element.29), channel_id=1, source_target_pairs={{0,2},{1,3},{2,0},{3,1},{4,8},{5,9},{6,10},{7,11},{8,4},{9,5},{10,... | collective-permute-start | bytes 651272 | tf_op jit(solution)/shard_map/ppermute | solution.py:435
  6.0 4.2 %collective-permute-start = (f32[112,128]{1,0:T(8,128)S(1)}, f32[112,128]{1,0:T(8,128)S(1)}, u32[]{:S(2)}, u32[]{:S(2)}) collective-permute-start(f32[112,128]{1,0:T(8,128)S(1)} %get-tuple-element.26), channel_id=1, source_target_pairs={{0,1},{1,0},{2,3},{3,2},{4,5},{5,4},{6,7},{7,6},{8,9},{9,8},{10,11... | collective-permute-start | bytes 172040 | tf_op jit(solution)/shard_map/ppermute | solution.py:435
  7.5 2.7 %collective-permute-start.1 = (f32[112,128]{1,0:T(8,128)S(1)}, f32[112,128]{1,0:T(8,128)S(1)}, u32[]{:S(2)}, u32[]{:S(2)}) collective-permute-start(f32[112,128]{1,0:T(8,128)S(1)} %get-tuple-element.27), channel_id=1, source_target_pairs={{0,4},{1,2},{2,1},{3,7},{4,0},{5,6},{6,5},{7,3},{8,12},{9,10},{10,... | collective-permute-start | bytes 172040 | tf_op jit(solution)/shard_map/ppermute | solution.py:435
  7.5 6.4 %collective-permute-start.4 = (f32[114,128]{1,0:T(8,128)S(1)}, f32[114,128]{1,0:T(8,128)S(1)}, u32[]{:S(2)}, u32[]{:S(2)}) collective-permute-start(f32[114,128]{1,0:T(8,128)S(1)} %get-tuple-element.30), channel_id=1, source_target_pairs={{0,1},{1,0},{2,3},{3,2},{4,5},{5,4},{6,7},{7,6},{8,9},{9,8},{10,11... | collective-permute-start | bytes 175112 | tf_op jit(solution)/shard_map/ppermute | solution.py:435
  10.2 3.7 %collective-permute-start.5 = (f32[114,128]{1,0:T(8,128)S(1)}, f32[114,128]{1,0:T(8,128)S(1)}, u32[]{:S(2)}, u32[]{:S(2)}) collective-permute-start(f32[114,128]{1,0:T(8,128)S(1)} %get-tuple-element.31), channel_id=1, source_target_pairs={{0,4},{1,2},{2,1},{3,7},{4,0},{5,6},{6,5},{7,3},{8,12},{9,10},{10,... | collective-permute-start | bytes 175112 | tf_op jit(solution)/shard_map/ppermute | solution.py:435
  10.3 3.8 %collective-permute-start.6 = (f32[114,128]{1,0:T(8,128)S(1)}, f32[114,128]{1,0:T(8,128)S(1)}, u32[]{:S(2)}, u32[]{:S(2)}) collective-permute-start(f32[114,128]{1,0:T(8,128)S(1)} %get-tuple-element.40), channel_id=1, source_target_pairs={{0,4},{1,5},{2,6},{3,7},{4,0},{5,1},{6,2},{7,3},{8,12},{9,13},{10,... | collective-permute-start | bytes 175112 | tf_op jit(solution)/shard_map/ppermute | solution.py:435
  10.9 5.3 %collective-permute-start.7 = (f32[114,128]{1,0:T(8,128)S(1)}, f32[114,128]{1,0:T(8,128)S(1)}, u32[]{:S(2)}, u32[]{:S(2)}) collective-permute-start(f32[114,128]{1,0:T(8,128)S(1)} %get-tuple-element.41), channel_id=1, source_target_pairs={{0,2},{1,3},{2,0},{3,1},{4,8},{5,9},{6,10},{7,11},{8,4},{9,5},{10,... | collective-permute-start | bytes 175112 | tf_op jit(solution)/shard_map/ppermute | solution.py:435
